TPU v7x, 32 devices: a whole 2x2x4 slice. The times are simulated.
32 devices in a mesh: segment: 4 (over x, core), ctx: 4 (over z), head: 2 (over y).
Axes of the slice: x: 2, y: 2, z: 4, core: 2. Of those that a mesh axis runs over, the one named last changes fastest.
Arguments:
- queries: bfloat16 [512, 8192], P('segment', 'head'), may hold values from -6 to 6
- keys: bfloat16 [65536, 1024], P(('segment', 'ctx'), 'head'), may hold values from -6 to 6
- values: bfloat16 [65536, 1024], P(('segment', 'ctx'), 'head'), may hold values from -6 to 6
- lengths: int32 [4], P('segment'), may hold values from 6145 to 16384, as said below
- selected: int32 [4, 3], P('segment'), may hold values from 0 to 7, as said below
- out_weight: bfloat16 [8192, 8192], P(('head', 'ctx')), may hold values from -3 to 3
Outputs:
- handed: bfloat16 [512, 8192], P('segment', ('head', 'ctx'))
Inputs may be any that keep to these rules, and one draw needn't show every extreme that they name: `lengths`: Even-indexed sections hold 8192 cached positions or fewer, odd-indexed ones more than 8192; some section holds exactly 16384. `selected`: each row names 3 distinct blocks, each holding at least one cached position of its section; block 0 and the block holding the section's last cached position are always named.
All inputs are finite; a program needn't handle non-finite values.
Results may differ from a plain program's by a relative error of at most 0.019.
Values may be sent and summed in bfloat16 or wider, within the bound.
A program may use at most 192 MiB of HBM per device.

v0:
```python
import functools
import math

import jax
import jax.numpy as jnp
from jax import lax
from jax.sharding import PartitionSpec as P

HEAD_DIM = 128
BLOCK = 2048


MASKED = -1e30


def shifted(value, axis, steps):
    count = lax.axis_size(axis)
    pairs = [(source, (source + steps) % count) for source in range(count)]
    return lax.ppermute(value, axis, pairs)


def attend_block(carry, query_heads, key_heads, value_heads, chosen, cached, offset, block_index):
    run_max, run_sum, run_out = carry
    first_row = block_index * BLOCK
    key_block = key_heads[first_row : first_row + BLOCK]
    value_block = value_heads[first_row : first_row + BLOCK]
    positions = offset + first_row + jnp.arange(BLOCK, dtype=jnp.int32)
    block_id = (offset + first_row) // BLOCK
    picked = jnp.any(chosen == block_id)
    usable = (positions < cached) & picked
    scores = jnp.einsum(
        "rkgd,pkd->rkgp", query_heads, key_block, preferred_element_type=jnp.float32
    )
    scores = scores * (1.0 / math.sqrt(HEAD_DIM))
    scores = jnp.where(usable[None, None, None, :], scores, MASKED)
    new_max = jnp.maximum(run_max, jnp.max(scores, axis=-1))
    expo = jnp.where(usable[None, None, None, :], jnp.exp(scores - new_max[..., None]), 0.0)
    factor = jnp.exp(run_max - new_max)
    run_sum = run_sum * factor + jnp.sum(expo, axis=-1)
    gathered = jnp.einsum(
        "rkgp,pkd->rkgd", expo.astype(jnp.bfloat16), value_block, preferred_element_type=jnp.float32
    )
    run_out = run_out * factor[..., None] + gathered
    return (new_max, run_sum, run_out)


def on_device(queries, keys, values, lengths, selected, out_weight):
    row_total = queries.shape[0]
    local_kv = keys.shape[1] // HEAD_DIM
    local_q = queries.shape[1] // HEAD_DIM
    heads_per_group = local_q // local_kv
    ctx_size = lax.axis_size("ctx")
    per_ctx = local_q // ctx_size
    key_span = keys.shape[0]
    offset = lax.axis_index("ctx") * key_span
    cached = lengths[0]
    chosen = selected[0]
    query_heads = queries.reshape(row_total, local_kv, heads_per_group, HEAD_DIM)
    key_heads = keys.reshape(key_span, local_kv, HEAD_DIM)
    value_heads = values.reshape(key_span, local_kv, HEAD_DIM)
    carry = (
        jnp.full((row_total, local_kv, heads_per_group), MASKED, jnp.float32),
        jnp.zeros((row_total, local_kv, heads_per_group), jnp.float32),
        jnp.zeros((row_total, local_kv, heads_per_group, HEAD_DIM), jnp.float32),
    )
    for block_index in range(key_span // BLOCK):
        step = functools.partial(
            attend_block,
            query_heads=query_heads,
            key_heads=key_heads,
            value_heads=value_heads,
            chosen=chosen,
            cached=cached,
            offset=offset,
            block_index=block_index,
        )
        carry = step(carry)
    run_max = carry[0].reshape(row_total, local_q)
    run_sum = carry[1].reshape(row_total, local_q)
    run_out = carry[2].reshape(row_total, local_q, HEAD_DIM)
    largest = lax.pmax(run_max, "ctx")
    factor = jnp.exp(run_max - largest)
    share_out, share_sum = (
        lax.psum_scatter(
            (run_out * factor[..., None]).astype(jnp.bfloat16),
            "ctx",
            scatter_dimension=1,
            tiled=True,
        ).astype(jnp.float32),
        lax.psum_scatter(
            (run_sum * factor).astype(jnp.bfloat16), "ctx", scatter_dimension=1, tiled=True
        ).astype(jnp.float32),
    )
    own_heads = (share_out / share_sum[..., None]).astype(jnp.bfloat16)
    own_flat = own_heads.reshape(row_total, per_ctx * HEAD_DIM)
    partial_cols = lax.psum_scatter(
        lax.dot_general(
            out_weight, own_flat, (((0,), (1,)), ((), ())), preferred_element_type=jnp.float32
        ),
        ("head", "ctx"),
        scatter_dimension=0,
        tiled=True,
    )
    finished = jnp.transpose(partial_cols).astype(jnp.bfloat16)
    return shifted(finished, "segment", 1)


def solution(mesh):
    placed = (
        P("segment", "head"),
        P(("segment", "ctx"), "head"),
        P(("segment", "ctx"), "head"),
        P("segment"),
        P("segment", None),
        P(("head", "ctx"), None),
    )
    return jax.shard_map(
        on_device,
        mesh=mesh,
        in_specs=placed,
        out_specs=P("segment", ("head", "ctx")),
        check_vma=False,
    )
```

profile of v0, /device:TPU:1, one launch (start us, length us, event | category | flops | bytes accessed | tf_op | source)
XLA Modules:
  0.0 290.4 jit_solution(7546012605706277077)
XLA Ops:
  6.5 0.0 copy-start.1
  6.5 0.0 reduce-scatter.3.cloned.1.call-start
  7.2 3.8 %fusion.39 = (bf16[2048,512]{1,0:T(8,128)(2,1)S(1)}, bf16[2048,512]{1,0:T(8,128)(2,1)}) fusion(bf16[4096,512]{1,0:T(8,128)(2,1)} %param.7), kind=kLoop, calls=%fused_computation.61 | loop fusion | bytes 8388608 | tf_op jit(solution)/shard_map/slice | solution.py:25
  11.0 2.5 copy.51
  13.6 1.4 copy.55
  15.0 2.9 %copy.53 = bf16[2048,512]{0,1:T(8,128)(2,1)S(1)} copy(bf16[2048,512]{1,0:T(8,128)(2,1)} %get-tuple-element.10) | data formatting | bytes 4194304
  18.0 0.0 copy-done.1
  18.0 0.7 compare_reduce_fusion.1
  18.7 1.3 fusion.29
  19.9 16.3 %bitcast_reduce_fusion.1 = (f32[128,4,8]{0,2,1:T(8,128)S(1)}, f32[4,2048,128,8]{2,1,3,0:T(8,128)}) fusion(pred[2048]{0:T(1024)(128)(4,1)S(1)} %get-tuple-element.21, bf16[2048,4,128,1]{0,2,3,1:T(8,128)(2,1)} %bitcast.103, bf16[128,4,8,128]{3,2,1,0:T(8,128)(2,1)S(1)} %bitcast.100), kind=kOutput, calls=%fused_computation.5 | convolution fusion | flops 2172645376 | bytes 36718592 | tf_op jit(solution)/shard_map/rkgd,pkd->rkgp/dot_general | solution.py:31
  36.3 14.7 %bitcast_reduce_fusion = (f32[128,4,8]{0,2,1:T(8,128)S(1)}, f32[4,2048,128,8]{2,1,3,0:T(8,128)}) fusion(pred[2048]{0:T(1024)(128)(4,1)S(1)} %get-tuple-element.22, bf16[2048,4,128,1]{0,2,3,1:T(8,128)(2,1)S(1)} %bitcast.102, bf16[128,4,8,128]{3,2,1,0:T(8,128)(2,1)S(1)} %bitcast.101), kind=kOutput, calls=%fused_computation.1 | convolution fusion | flops 2172645376 | bytes 36718592 | tf_op jit(solution)/shard_map/rkgd,pkd->rkgp/dot_general | solution.py:31
  51.0 16.1 %pmax.7 = f32[128,32]{0,1:T(8,128)S(1)} all-reduce(f32[128,32]{0,1:T(8,128)S(1)} %bitcast_maximum_fusion), channel_id=1, replica_groups=mesh['segment'=4,'ctx'=4,'head'=2] {'ctx'}, use_global_device_ids=true, to_apply=%region_4.5 | all-reduce | flops 4096 | bytes 32768 | tf_op jit(solution)/shard_map/pmax | solution.py:81
  67.1 3.8 %fusion.38 = (bf16[2048,512]{1,0:T(8,128)(2,1)S(1)}, bf16[2048,512]{1,0:T(8,128)(2,1)}) fusion(bf16[4096,512]{1,0:T(8,128)(2,1)} %param.8), kind=kLoop, calls=%fused_computation.60 | loop fusion | bytes 8388608 | tf_op jit(solution)/shard_map/slice | solution.py:26
  70.9 4.0 %copy.54 = bf16[2048,512]{0,1:T(8,128)(2,1)} copy(bf16[2048,512]{1,0:T(8,128)(2,1)} %get-tuple-element.8) | data formatting | bytes 4194304
  74.9 15.3 %fusion.6 = f32[128,4,8]{0,2,1:T(8,128)S(1)} fusion(f32[4,2048,128,8]{2,1,3,0:T(8,128)} %get-tuple-element.20, f32[128,4,8]{0,2,1:T(8,128)S(1)} %get-tuple-element.14, pred[2048]{0:T(1024)(128)(4,1)S(1)} %get-tuple-element.22), kind=kLoop, calls=%fused_computation.12 | loop fusion | flops 41938944 | bytes 33589248 | tf_op jit(solution)/shard_map/reduce_sum | solution.py:39
  90.2 18.7 %fusion.8 = f32[4,128,8,128]{3,1,2,0:T(8,128)} fusion(bf16[2048,4,128,1]{0,2,3,1:T(8,128)(2,1)} %bitcast.106, f32[4,2048,128,8]{2,1,3,0:T(8,128)} %get-tuple-element.20, f32[128,4,8]{0,2,1:T(8,128)S(1)} %get-tuple-element.14, pred[2048]{0:T(1024)(128)(4,1)S(1)} %get-tuple-element.22), kind=kOutput, calls=%fused_computation.14 | convolution fusion | flops 2189426688 | bytes 37767168 | tf_op jit(solution)/shard_map/rkgp,pkd->rkgd/dot_general | solution.py:40
  108.9 2.5 copy.52
  111.5 0.0 copy-start
  111.5 0.0 copy-start.3
  111.5 15.6 %fusion.4 = f32[128,4,8]{0,2,1:T(8,128)S(1)} fusion(f32[4,2048,128,8]{2,1,3,0:T(8,128)} %get-tuple-element.18, f32[128,4,8]{0,2,1:T(8,128)S(1)} %get-tuple-element.16, pred[2048]{0:T(1024)(128)(4,1)S(1)} %get-tuple-element.21), kind=kLoop, calls=%fused_computation.10 | loop fusion | flops 41938944 | bytes 33589248 | tf_op jit(solution)/shard_map/reduce_sum | solution.py:39
  127.1 0.0 copy-done
  127.1 0.0 copy-done.3
  127.1 0.0 copy-start.2
  127.1 18.7 %bitcast_add_fusion = f32[128,4,8,128]{3,0,2,1:T(8,128)} fusion(f32[4,128,8,128]{3,1,2,0:T(8,128)S(1)} %copy-done.3, bf16[2048,4,128,1]{0,2,3,1:T(8,128)(2,1)S(1)} %bitcast.104, f32[4,2048,128,8]{2,1,3,0:T(8,128)} %get-tuple-element.18, f32[128,4,8]{0,2,1:T(8,128)S(1)} %get-tuple-element.16, pred[2048]{0:T(1024)(128)(4,1)S(1)} %get-tuple-element.21, ...), kind=kOutput, calls=%fused_computation.21 | convolution fusion | flops 2190999552 | bytes 39897088 | tf_op jit(solution)/shard_map/rkgp,pkd->rkgd/dot_general | solution.py:40
  145.8 1.9 copy.36
  147.7 1.3 multiply_convert_fusion
  149.0 0.0 reduce-scatter.3.cloned.1.call-update
  149.0 0.0 reduce-scatter.5.cloned.1.call-start
  149.1 0.0 copy-done.2
  149.1 0.6 dynamic-slice
  150.3 6.8 %all-reduce = bf16[128,32]{0,1:T(8,128)(2,1)S(1)} all-reduce(bf16[128,32]{0,1:T(8,128)(2,1)S(1)} %get-tuple-element.11), channel_id=3, replica_groups=mesh['segment'=4,'ctx'=4,'head'=2] {'ctx'}, use_global_device_ids=true, to_apply=%region_8.9.clone | all-reduce | flops 4096 | bytes 16384
  157.1 21.1 %reduce-scatter.3.cloned.1.call-done = bf16[128,8,128]{0,2,1:T(8,128)(2,1)} async-done(((bf16[128,32,128]{0,2,1:T(8,128)(2,1)}), bf16[128,8,128]{0,2,1:T(8,128)(2,1)}) %reduce-scatter.3.cloned.1.call-update) | async-done | bytes 262160 | tf_op jit(solution)/shard_map/reduce_scatter | solution.py:84
  178.2 1.0 divide_convert_fusion
  179.2 10.2 %convolution_bitcast_fusion = f32[8192,128]{0,1:T(8,128)} fusion(bf16[128,1024]{0,1:T(8,128)(2,1)S(1)} %bitcast.108, bf16[1024,8192]{1,0:T(8,128)(2,1)} %param.11), kind=kOutput, calls=%fused_computation.20 | convolution fusion | flops 2147483648 | bytes 21233664 | tf_op jit(solution)/shard_map/dot_general | solution.py:97
  189.4 0.0 reduce-scatter.5.cloned.1.call-update
  189.4 87.3 %reduce-scatter.5.cloned.1.call-done = f32[1024,128]{0,1:T(8,128)} async-done(((f32[8192,128]{0,1:T(8,128)}), f32[1024,128]{0,1:T(8,128)}) %reduce-scatter.5.cloned.1.call-update) | async-done | bytes 524304 | tf_op jit(solution)/shard_map/reduce_scatter | solution.py:96
  276.7 1.1 convert_bitcast_fusion
  277.8 1.7 collective-permute-start
  279.6 3.3 %collective-permute-done = bf16[128,1024]{1,0:T(8,128)(2,1)S(1)} collective-permute-done((bf16[128,1024]{1,0:T(8,128)(2,1)S(1)}, bf16[128,1024]{1,0:T(8,128)(2,1)S(1)}, u32[]{:S(2)}, u32[]{:S(2)}) %collective-permute-start) | collective-permute-done | bytes 262176 | tf_op jit(solution)/shard_map/ppermute | solution.py:19
  282.9 0.7 copy.66
  (4 shorter events, 0.1 us)
Async XLA Ops:
  6.5 11.4 %copy-start.1 = (s32[1,3]{1,0:T(1,128)S(1)}, s32[1,3]{1,0:T(1,128)}, u32[]{:S(2)}) copy-start(s32[1,3]{1,0:T(1,128)} %param.10) | copy-start | bytes 40
  6.5 171.6 %reduce-scatter.3.cloned.1.call-start = ((), (), s32[]{:S(2)}) async-start(), calls=%async_computation.2 | async-start | bytes 1310720 | tf_op jit(solution)/shard_map/reduce_scatter | solution.py:84
  111.5 15.6 %copy-start = (bf16[2048,512]{0,1:T(8,128)(2,1)S(1)}, bf16[2048,512]{0,1:T(8,128)(2,1)}, u32[]{:S(2)}) copy-start(bf16[2048,512]{0,1:T(8,128)(2,1)} %copy.52) | copy-start | bytes 6291460
  111.5 15.6 %copy-start.3 = (f32[4,128,8,128]{3,1,2,0:T(8,128)S(1)}, f32[4,128,8,128]{3,1,2,0:T(8,128)}, u32[]{:S(2)}) copy-start(f32[4,128,8,128]{3,1,2,0:T(8,128)} %fusion.8) | copy-start | bytes 6291460
  127.1 22.0 %copy-start.2 = (u32[32]{0:T(128)S(1)}, u32[32]{0:T(128)}, u32[]{:S(2)}) copy-start(u32[32]{0:T(128)} %constant.49) | copy-start | bytes 388
  149.0 127.7 %reduce-scatter.5.cloned.1.call-start = ((), (), s32[]{:S(2)}) async-start(), calls=%async_computation.3 | async-start | bytes 4718592 | tf_op jit(solution)/shard_map/reduce_scatter | solution.py:96
  277.8 5.1 %collective-permute-start = (bf16[128,1024]{1,0:T(8,128)(2,1)S(1)}, bf16[128,1024]{1,0:T(8,128)(2,1)S(1)}, u32[]{:S(2)}, u32[]{:S(2)}) collective-permute-start(bf16[128,1024]{1,0:T(8,128)(2,1)S(1)} %convert_bitcast_fusion), channel_id=1, source_target_pairs={{0,8},{8,16},{16,24},{24,0},{1,9},{9,17},{17,25},{25,1},{2,10},{10... | collective-permute-start | bytes 786440 | tf_op jit(solution)/shard_map/ppermute | solution.py:19
Sparse Core Ops, SparseCore 0:
  149.1 29.0 reduce-scatter.2
  189.5 87.1 reduce-scatter.4
where the time goes:
time: 293 us; the launch traced here: 290 us
  waiting for transfers between devices  112 us (38%)
  matrix products  78.6 us (27%)
  other arithmetic  36.3 us (12%)
  local copies, waits for them, and re-layouts  24.3 us (8%)
  blocking collectives  22.9 us (8%)
  between operations  14.9 us (5%)
    reduce_scatter x1, waiting for transfers between devices, on_device(): lax.psum_scatter(lax.dot_general(out_weight, own_flat, (((0,), (1,)), (()...  87.3 us
    dot_general x2, matrix products, attend_block(): jnp.einsum('rkgp,pkd->rkgd', expo.astype(jnp.bfloat16), value_block, pref...  37.4 us
    dot_general x2, matrix products, attend_block(): jnp.einsum('rkgd,pkd->rkgp', query_heads, key_block, preferred_element_ty...  31 us
    reduce_sum x2, other arithmetic, attend_block(): run_sum = run_sum * factor + jnp.sum(expo, axis=-1)  30.9 us
    reduce_scatter x1, waiting for transfers between devices, on_device(): lax.psum_scatter((run_out * factor[..., None]).astype(jnp.bfloat16), 'ctx...  21.1 us
    pmax x1, blocking collectives, on_device(): largest = lax.pmax(run_max, 'ctx')  16.1 us
    unnamed x15, local copies, waits for them, and re-layouts  14.7 us
    dot_general x1, matrix products, on_device(): lax.dot_general(out_weight, own_flat, (((0,), (1,)), ((), ())), preferred...  10.2 us
  transfers between devices with their start and end apart: 3, of which 3 were waited for; matrix products, arithmetic and copies ran while one was open for 0% of the time, Pallas kernels for 0%

commit v1 on v0

v1 whole, which is shorter than its diff:
```python
import functools
import math

import jax
import jax.numpy as jnp
from jax import lax
from jax.experimental import pallas as pl
from jax.experimental.pallas import tpu as pltpu
from jax.sharding import PartitionSpec as P

HEAD_DIM = 128
BLOCK = 2048
MASKED = -1e30
FLOOR = -1e20
UNITS = math.log2(math.e) / math.sqrt(HEAD_DIM)
MESH = pl.DeviceIdType.MESH


def relay(
    sizes,
    length_ref,
    chosen_ref,
    q_hbm,
    k_hbm,
    v_hbm,
    w_hbm,
    out_ref,
    q_buf,
    k_buf,
    v_buf,
    w_buf,
    bias,
    a_send,
    a_recv,
    t_send,
    t_recv,
    attn,
    y_send,
    y_recv,
    z_send,
    z_recv,
    load_sem,
    k_sem,
    v_sem,
    a_sems,
    t_sems,
    y_sems,
    z_sems,
):
    S, C, H = sizes
    seg, ctx, head = lax.axis_index("segment"), lax.axis_index("ctx"), lax.axis_index("head")
    rows, q_cols = q_buf.shape
    kv_count, span, _ = k_buf.shape
    per_ctx = q_cols // (HEAD_DIM * C)
    group = q_cols // (HEAD_DIM * kv_count)
    together = 2 if per_ctx % 2 == 0 else 1
    width = out_ref.shape[1]
    stat_rows = t_send.shape[1]
    aligned = kv_count == C

    barrier = pltpu.get_barrier_semaphore()

    def greet(s, c, h):
        pl.semaphore_signal(barrier, inc=1, device_id=(s, c, h), device_id_type=MESH)

    for k in range(1, C):
        greet(seg, lax.rem(ctx + k, C), head)
    for k in range(1, H):
        greet(seg, ctx, lax.rem(head + k, H))
    for k in range(C):
        greet(lax.rem(seg + S - 1, S), lax.rem(ctx + k, C), head)

    def load_q():
        return pltpu.make_async_copy(q_hbm, q_buf, load_sem.at[0])

    def load_w():
        return pltpu.make_async_copy(w_hbm, w_buf, load_sem.at[1])

    def load_kv(i):
        which = lax.rem(ctx + 1 + i, C) if aligned else i
        columns = pl.ds(pl.multiple_of(which * HEAD_DIM, HEAD_DIM), HEAD_DIM)
        return (
            pltpu.make_async_copy(k_hbm.at[:, columns], k_buf.at[i], k_sem.at[i]),
            pltpu.make_async_copy(v_hbm.at[:, columns], v_buf.at[i], v_sem.at[i]),
        )

    load_q().start()
    for i in range(kv_count):
        for copy in load_kv(i):
            copy.start()
    load_w().start()

    length = length_ref[0]
    for b in range(span // BLOCK):
        first = ctx * span + b * BLOCK
        picked = jnp.int32(0)
        for i in range(chosen_ref.shape[1]):
            picked = jnp.where(chosen_ref[0, i] == first // BLOCK, 1, picked)
        limit = jnp.where(picked == 1, length, 0)
        place = first + lax.broadcasted_iota(jnp.int32, (8, BLOCK), 1)
        bias[:, b * BLOCK : (b + 1) * BLOCK] = jnp.where(place < limit, 0.0, MASKED)

    load_q().wait()
    if not aligned:
        for i in range(kv_count):
            for copy in load_kv(i):
                copy.wait()

    def a_copies(k):
        to = (seg, lax.rem(ctx + 1 + k, C), head)
        return (
            pltpu.make_async_remote_copy(
                src_ref=a_send.at[k], dst_ref=a_recv.at[k], send_sem=a_sems.at[0, k],
                recv_sem=a_sems.at[1, k], device_id=to, device_id_type=MESH,
            ),
            pltpu.make_async_remote_copy(
                src_ref=t_send.at[k], dst_ref=t_recv.at[k], send_sem=t_sems.at[0, k],
                recv_sem=t_sems.at[1, k], device_id=to, device_id_type=MESH,
            ),
        )

    lane = lax.broadcasted_iota(jnp.int32, (rows, HEAD_DIM), 1)

    def unit(k, carry):
        owner = lax.rem(ctx + 1 + k, C)
        if aligned:
            slot = k
            for copy in load_kv(k):
                copy.wait()
        else:
            slot = (owner * per_ctx) // group

        def heads(t, stats):
            at = pl.multiple_of((owner * per_ctx + t * together) * HEAD_DIM, HEAD_DIM)
            q = jnp.concatenate(
                [
                    q_buf[:, pl.ds(pl.multiple_of(at + i * HEAD_DIM, HEAD_DIM), HEAD_DIM)]
                    for i in range(together)
                ],
                axis=0,
            )
            scores = lax.dot_general(
                q, k_buf[slot], (((1,), (1,)), ((), ())), preferred_element_type=jnp.float32
            )
            scores = scores + bias[0:1, :]
            top = jnp.maximum(jnp.max(scores, axis=1, keepdims=True), FLOOR)
            expo = jnp.exp2(scores * UNITS - top * UNITS).astype(jnp.bfloat16)
            ones = jnp.ones((span, HEAD_DIM), jnp.bfloat16)
            summed = jnp.dot(
                expo,
                jnp.concatenate([v_buf[slot], ones], axis=1),
                preferred_element_type=jnp.float32,
            )
            for i in range(together):
                part = slice(i * rows, (i + 1) * rows)
                j = t * together + i
                dst = pl.multiple_of(j * HEAD_DIM, HEAD_DIM)
                a_send[k, :, pl.ds(dst, HEAD_DIM)] = summed[part, :HEAD_DIM].astype(jnp.bfloat16)
                stats = jnp.where(lane == j, top[part], stats)
                stats = jnp.where(lane == per_ctx + j, summed[part, HEAD_DIM:], stats)
            return stats

        stats = lax.fori_loop(
            0, per_ctx // together, heads, jnp.zeros((rows, HEAD_DIM), jnp.float32)
        )
        t_send[k] = jnp.transpose(stats)[:stat_rows]

        @pl.when(k == 0)
        def _():
            pl.semaphore_wait(barrier, 2 * C + H - 2)

        @pl.when(k < C - 1)
        def _():
            for copy in a_copies(k):
                copy.start()

        return carry

    lax.fori_loop(0, C, unit, 0)

    for k in range(C - 1):
        for copy in a_copies(k):
            copy.wait()
    load_w().wait()

    def column_form(block):
        fill = jnp.zeros((HEAD_DIM - stat_rows, rows), jnp.float32)
        return jnp.transpose(jnp.concatenate([block, fill], axis=0))

    stats = [column_form(t_recv[k]) for k in range(C - 1)] + [column_form(t_send[C - 1])]
    tops = [s[:, :per_ctx] for s in stats]
    sums = [s[:, per_ctx : 2 * per_ctx] for s in stats]
    largest = functools.reduce(jnp.maximum, tops)
    factors = [jnp.exp2((top - largest) * UNITS) for top in tops]
    total = functools.reduce(jnp.add, [f * s for f, s in zip(factors, sums)])
    factors = [f / total for f in factors]
    for j in range(per_ctx):
        part = slice(j * HEAD_DIM, (j + 1) * HEAD_DIM)
        shares = [a_recv[k, :, part] for k in range(C - 1)] + [a_send[C - 1, :, part]]
        joined = functools.reduce(
            jnp.add,
            [f[:, j : j + 1] * share.astype(jnp.float32) for f, share in zip(factors, shares)],
        )
        attn[:, part] = joined.astype(jnp.bfloat16)

    def columns_of(h, k):
        c = lax.rem(ctx + 1 + k, C)
        start = pl.multiple_of((h * C + c) * width, width)
        return jnp.dot(attn[...], w_buf[:, pl.ds(start, width)], preferred_element_type=jnp.float32)

    def y_copy(i, k):
        return pltpu.make_async_remote_copy(
            src_ref=y_send.at[i, k], dst_ref=y_recv.at[i, k], send_sem=y_sems.at[0, i, k],
            recv_sem=y_sems.at[1, i, k], device_id=(seg, ctx, lax.rem(head + 1 + i, H)),
            device_id_type=MESH,
        )

    def z_copy(k):
        return pltpu.make_async_remote_copy(
            src_ref=z_send.at[k], dst_ref=z_recv.at[k], send_sem=z_sems.at[0, k],
            recv_sem=z_sems.at[1, k],
            device_id=(lax.rem(seg + 1, S), lax.rem(ctx + 1 + k, C), head),
            device_id_type=MESH,
        )

    def outgoing(n, carry):
        k, i = n // (H - 1), n % (H - 1)
        y_send[i, k] = columns_of(lax.rem(head + 1 + i, H), k).astype(jnp.bfloat16)
        y_copy(i, k).start()
        return carry

    lax.fori_loop(0, C * (H - 1), outgoing, 0)

    def passed_on(k, carry):
        mine = columns_of(head, k)
        for i in range(H - 1):
            y_copy(i, k).wait()
            mine = mine + y_recv[i, k].astype(jnp.float32)
        z_send[k] = mine.astype(jnp.bfloat16)
        z_copy(k).start()
        return carry

    lax.fori_loop(0, C, passed_on, 0)

    result = jnp.zeros(out_ref.shape, jnp.float32)
    for k in range(C):
        z_copy(k).wait()
        result = result + z_recv[k].astype(jnp.float32)
    out_ref[...] = result.astype(out_ref.dtype)


def on_device(queries, keys, values, lengths, selected, out_weight):
    S, C, H = lax.axis_size("segment"), lax.axis_size("ctx"), lax.axis_size("head")
    rows, q_cols = queries.shape
    span, kv_cols = keys.shape
    kv_count = kv_cols // HEAD_DIM
    depth, d = out_weight.shape
    width = d // (C * H)
    stat_rows = -(-2 * (depth // HEAD_DIM) // 8) * 8
    whole = pl.BlockSpec(memory_space=pl.ANY)
    scalars = pl.BlockSpec(memory_space=pltpu.SMEM)
    wire = jnp.bfloat16
    return pl.pallas_call(
        functools.partial(relay, (S, C, H)),
        out_shape=jax.ShapeDtypeStruct((rows, width), jnp.bfloat16),
        in_specs=[scalars, scalars, whole, whole, whole, whole],
        out_specs=pl.BlockSpec(memory_space=pltpu.VMEM),
        scratch_shapes=[
            pltpu.VMEM((rows, q_cols), queries.dtype),
            pltpu.VMEM((kv_count, span, HEAD_DIM), keys.dtype),
            pltpu.VMEM((kv_count, span, HEAD_DIM), values.dtype),
            pltpu.VMEM((depth, d), out_weight.dtype),
            pltpu.VMEM((8, span), jnp.float32),
            pltpu.VMEM((C, rows, depth), wire),
            pltpu.VMEM((C - 1, rows, depth), wire),
            pltpu.VMEM((C, stat_rows, rows), jnp.float32),
            pltpu.VMEM((C - 1, stat_rows, rows), jnp.float32),
            pltpu.VMEM((rows, depth), wire),
            pltpu.VMEM((H - 1, C, rows, width), wire),
            pltpu.VMEM((H - 1, C, rows, width), wire),
            pltpu.VMEM((C, rows, width), wire),
            pltpu.VMEM((C, rows, width), wire),
            pltpu.SemaphoreType.DMA((2,)),
            pltpu.SemaphoreType.DMA((kv_count,)),
            pltpu.SemaphoreType.DMA((kv_count,)),
            pltpu.SemaphoreType.DMA((2, C - 1)),
            pltpu.SemaphoreType.DMA((2, C - 1)),
            pltpu.SemaphoreType.DMA((2, H - 1, C)),
            pltpu.SemaphoreType.DMA((2, C)),
        ],
        compiler_params=pltpu.CompilerParams(
            collective_id=0, has_side_effects=True, vmem_limit_bytes=58 * 2**20
        ),
        cost_estimate=pl.CostEstimate(
            flops=4 * rows * q_cols * span + 2 * rows * depth * d,
            bytes_accessed=2 * (rows * q_cols + 2 * span * kv_cols + depth * d),
            transcendentals=rows * q_cols // HEAD_DIM * span,
        ),
    )(lengths, selected, queries, keys, values, out_weight)


def solution(mesh):
    placed = (
        P("segment", "head"),
        P(("segment", "ctx"), "head"),
        P(("segment", "ctx"), "head"),
        P("segment"),
        P("segment", None),
        P(("head", "ctx"), None),
    )
    return jax.shard_map(
        on_device,
        mesh=mesh,
        in_specs=placed,
        out_specs=P("segment", ("head", "ctx")),
        check_vma=False,
    )
```

time: 293 us -> 91.8 us (0.31)
  waiting for transfers between devices: 112 us -> 0 us
  Pallas kernels: 0 us -> 88.2 us
  matrix products: 78.6 us -> 0 us
  other arithmetic: 36.3 us -> 0 us
  blocking collectives: 22.9 us -> 0 us
  local copies, waits for them, and re-layouts: 24.3 us -> 1.67 us
  between operations: 14.9 us -> 0.66 us
    reduce_scatter x2 -> x0, waiting for transfers between devices: 108 us -> none  [the longest x1 87.3 us: on_device(): lax.psum_scatter(lax.dot_general(out_weight, own_flat, (((0,), (1,)), (()...]
    pallas_call x0 -> x1, Pallas kernels: none -> 88.2 us  [on_device(): pl.pallas_call(functools.partial(relay, (S, C, H)), out_shape=jax.ShapeDt...]
    dot_general x5 -> x0, matrix products: 78.6 us -> none  [the longest x2 37.4 us: attend_block(): jnp.einsum('rkgp,pkd->rkgd', expo.astype(jnp.bfloat16), value_block, pref...]
    reduce_sum x2 -> x0, other arithmetic: 30.9 us -> none  [attend_block(): run_sum = run_sum * factor + jnp.sum(expo, axis=-1)]
    pmax x1 -> x0, blocking collectives: 16.1 us -> none  [on_device(): largest = lax.pmax(run_max, 'ctx')]
    unnamed x15 -> x1, local copies, waits for them, and re-layouts: 14.7 us -> 1.67 us
    slice x2 -> x0, local copies, waits for them, and re-layouts: 7.67 us -> none  [the longest x1 3.84 us: attend_block(): key_block = key_heads[first_row:first_row + BLOCK]]
    unnamed x1 -> x0, blocking collectives: 6.79 us -> none
  transfers between devices with their start and end apart: 3 -> 0, of which waited for: 3 -> 0; matrix products, arithmetic and copies ran while one was open for 0% -> 0% of each run, Pallas kernels for 0% -> 0%
where the time goes in v1:
time: 91.8 us; the launch traced here: 90.5 us
  Pallas kernels  88.2 us (96%)
  local copies, waits for them, and re-layouts  1.67 us (2%)
    pallas_call x1, Pallas kernels, on_device(): pl.pallas_call(functools.partial(relay, (S, C, H)), out_shape=jax.ShapeDt...  88.2 us

profile of v1, /device:TPU:1, one launch (start us, length us, event | category | flops | bytes accessed | tf_op | source)
XLA Modules:
  0.0 90.5 jit_solution(110557934488081562)
XLA Ops:
  0.7 88.2 %shard_map.64 = bf16[128,1024]{1,0:T(8,128)(2,1)} custom-call(s32[1]{0:T(128)S(6)} %copy.8.length_ref, s32[1,3]{1,0:T(1,128)} %chosen_ref.1, bf16[128,4096]{1,0:T(8,128)(2,1)} %q_hbm.1, bf16[4096,512]{1,0:T(8,128)(2,1)} %k_hbm.1, bf16[4096,512]{1,0:T(8,128)(2,1)} %v_hbm.1, bf16[1024,8192]{1,0:T(8,128)(2,1)} %w_hbm.1), custom_call_target="tpu_custom_call" | custom-call | flops 10737418240 | bytes 26214400 | tf_op jit(solution)/shard_map/pallas_call | solution.py:263
  88.9 1.7 %copy.9 = bf16[128,1024]{1,0:T(8,128)(2,1)} copy(bf16[128,1024]{1,0:T(8,128)(2,1)} %shard_map.64) | data formatting | bytes 524288

commit v2 on v1

v2 whole, which is shorter than its diff:
```python
import functools
import math

import jax
import jax.numpy as jnp
from jax import lax
from jax.experimental import pallas as pl
from jax.experimental.pallas import tpu as pltpu
from jax.sharding import PartitionSpec as P

HEAD_DIM = 128
BLOCK = 2048
MASKED = -1e30
FLOOR = -1e20
UNITS = math.log2(math.e) / math.sqrt(HEAD_DIM)
MESH = pl.DeviceIdType.MESH


def relay(
    sizes,
    length_ref,
    chosen_ref,
    q_hbm,
    k_hbm,
    v_hbm,
    w_hbm,
    out_ref,
    q_buf,
    k_buf,
    v_buf,
    w_buf,
    bias,
    a_send,
    a_recv,
    t_send,
    t_recv,
    attn,
    y_send,
    y_recv,
    z_send,
    z_recv,
    load_sem,
    k_sem,
    v_sem,
    a_sems,
    t_sems,
    y_sems,
    z_sems,
):
    S, C, H = sizes
    seg, ctx, head = lax.axis_index("segment"), lax.axis_index("ctx"), lax.axis_index("head")
    rows, q_cols = q_buf.shape
    kv_count, span, _ = k_buf.shape
    per_ctx = q_cols // (HEAD_DIM * C)
    group = q_cols // (HEAD_DIM * kv_count)
    together = math.gcd(per_ctx, 4)
    half = rows // 2
    width = out_ref.shape[1]
    stat_rows = t_send.shape[2]
    aligned = kv_count == C

    barrier = pltpu.get_barrier_semaphore()

    def greet(s, c, h):
        pl.semaphore_signal(barrier, inc=1, device_id=(s, c, h), device_id_type=MESH)

    for k in range(1, C):
        greet(seg, lax.rem(ctx + k, C), head)
    for k in range(1, H):
        greet(seg, ctx, lax.rem(head + k, H))
    for k in range(C):
        greet(lax.rem(seg + S - 1, S), lax.rem(ctx + k, C), head)

    def load_q():
        return pltpu.make_async_copy(q_hbm, q_buf, load_sem.at[0])

    def load_w():
        return pltpu.make_async_copy(w_hbm, w_buf, load_sem.at[1])

    def load_kv(i):
        which = lax.rem(ctx + 1 + i, C) if aligned else i
        columns = pl.ds(pl.multiple_of(which * HEAD_DIM, HEAD_DIM), HEAD_DIM)
        return (
            pltpu.make_async_copy(k_hbm.at[:, columns], k_buf.at[i], k_sem.at[i]),
            pltpu.make_async_copy(v_hbm.at[:, columns], v_buf.at[i], v_sem.at[i]),
        )

    load_q().start()
    for i in range(kv_count):
        for copy in load_kv(i):
            copy.start()
    load_w().start()

    length = length_ref[0]
    for b in range(span // BLOCK):
        first = ctx * span + b * BLOCK
        picked = jnp.int32(0)
        for i in range(chosen_ref.shape[1]):
            picked = jnp.where(chosen_ref[0, i] == first // BLOCK, 1, picked)
        limit = jnp.where(picked == 1, length, 0)
        place = first + lax.broadcasted_iota(jnp.int32, (8, BLOCK), 1)
        bias[:, b * BLOCK : (b + 1) * BLOCK] = jnp.where(place < limit, 0.0, MASKED)

    load_q().wait()
    if not aligned:
        for i in range(kv_count):
            for copy in load_kv(i):
                copy.wait()

    def a_copies(g, k):
        to = (seg, lax.rem(ctx + 1 + k, C), head)
        return (
            pltpu.make_async_remote_copy(
                src_ref=a_send.at[g, k], dst_ref=a_recv.at[g, k], send_sem=a_sems.at[0, g, k],
                recv_sem=a_sems.at[1, g, k], device_id=to, device_id_type=MESH,
            ),
            pltpu.make_async_remote_copy(
                src_ref=t_send.at[g, k], dst_ref=t_recv.at[g, k], send_sem=t_sems.at[0, g, k],
                recv_sem=t_sems.at[1, g, k], device_id=to, device_id_type=MESH,
            ),
        )

    lane = lax.broadcasted_iota(jnp.int32, (half, HEAD_DIM), 1)

    def unit(g, k):
        owner = lax.rem(ctx + 1 + k, C)
        slot = k if aligned else (owner * per_ctx) // group
        own_rows = pl.ds(pl.multiple_of(g * half, half), half)
        tiles = per_ctx // together
        scores = []
        for t in range(tiles):
            q = jnp.concatenate(
                [
                    q_buf[
                        own_rows,
                        pl.ds(
                            pl.multiple_of(
                                (owner * per_ctx + t * together + i) * HEAD_DIM, HEAD_DIM
                            ),
                            HEAD_DIM,
                        ),
                    ]
                    for i in range(together)
                ],
                axis=0,
            )
            scores.append(
                lax.dot_general(
                    q, k_buf[slot], (((1,), (1,)), ((), ())), preferred_element_type=jnp.float32
                )
                + bias[0:1, :]
            )
        stats = jnp.zeros((half, HEAD_DIM), jnp.float32)
        for t in range(tiles):
            top = jnp.maximum(jnp.max(scores[t], axis=1, keepdims=True), FLOOR)
            expo = jnp.exp2(scores[t] * UNITS - top * UNITS).astype(jnp.bfloat16)
            ones = jnp.ones((span, HEAD_DIM), jnp.bfloat16)
            summed = jnp.dot(
                expo,
                jnp.concatenate([v_buf[slot], ones], axis=1),
                preferred_element_type=jnp.float32,
            )
            for i in range(together):
                part = slice(i * half, (i + 1) * half)
                j = t * together + i
                a_send[g, k, :, j * HEAD_DIM : (j + 1) * HEAD_DIM] = summed[
                    part, :HEAD_DIM
                ].astype(jnp.bfloat16)
                stats = jnp.where(lane == j, top[part], stats)
                stats = jnp.where(lane == per_ctx + j, summed[part, HEAD_DIM:], stats)
        fill = jnp.zeros((HEAD_DIM - half, HEAD_DIM), jnp.float32)
        t_send[g, k] = jnp.transpose(jnp.concatenate([stats, fill], axis=0))[:stat_rows]

    def column_form(block):
        fill = jnp.zeros((HEAD_DIM - stat_rows, HEAD_DIM), jnp.float32)
        return jnp.transpose(jnp.concatenate([block, fill], axis=0))[:half]

    def combine(g):
        for k in range(C - 1):
            for copy in a_copies(g, k):
                copy.wait()
        stats = [column_form(t_recv[g, k]) for k in range(C - 1)]
        stats.append(column_form(t_send[g, C - 1]))
        tops = [s[:, :per_ctx] for s in stats]
        sums = [s[:, per_ctx : 2 * per_ctx] for s in stats]
        largest = functools.reduce(jnp.maximum, tops)
        factors = [jnp.exp2((top - largest) * UNITS) for top in tops]
        total = functools.reduce(jnp.add, [f * s for f, s in zip(factors, sums)])
        factors = [f / total for f in factors]
        for j in range(per_ctx):
            part = slice(j * HEAD_DIM, (j + 1) * HEAD_DIM)
            shares = [a_recv[g, k, :, part] for k in range(C - 1)] + [a_send[g, C - 1, :, part]]
            joined = functools.reduce(
                jnp.add,
                [f[:, j : j + 1] * share.astype(jnp.float32) for f, share in zip(factors, shares)],
            )
            attn[g, :, part] = joined.astype(jnp.bfloat16)

    def columns_of(g, h, k):
        c = lax.rem(ctx + 1 + k, C)
        start = pl.multiple_of((h * C + c) * width, width)
        return jnp.dot(attn[g], w_buf[:, pl.ds(start, width)], preferred_element_type=jnp.float32)

    def y_copy(g, i, k):
        return pltpu.make_async_remote_copy(
            src_ref=y_send.at[g, i, k], dst_ref=y_recv.at[g, i, k], send_sem=y_sems.at[0, g, i, k],
            recv_sem=y_sems.at[1, g, i, k], device_id=(seg, ctx, lax.rem(head + 1 + i, H)),
            device_id_type=MESH,
        )

    def z_copy(g, k):
        return pltpu.make_async_remote_copy(
            src_ref=z_send.at[g, k], dst_ref=z_recv.at[g, k], send_sem=z_sems.at[0, g, k],
            recv_sem=z_sems.at[1, g, k],
            device_id=(lax.rem(seg + 1, S), lax.rem(ctx + 1 + k, C), head),
            device_id_type=MESH,
        )

    def outgoing(g):
        def step(n, carry):
            k, i = n // (H - 1), n % (H - 1)
            y_send[g, i, k] = columns_of(g, lax.rem(head + 1 + i, H), k).astype(jnp.bfloat16)
            y_copy(g, i, k).start()
            return carry

        lax.fori_loop(0, C * (H - 1), step, 0)

    def pass_on(g, first, last):
        def step(k, carry):
            mine = columns_of(g, head, k)
            for i in range(H - 1):
                y_copy(g, i, k).wait()
                mine = mine + y_recv[g, i, k].astype(jnp.float32)
            z_send[g, k] = mine.astype(jnp.bfloat16)
            z_copy(g, k).start()
            return carry

        lax.fori_loop(first, last, step, 0)

    def turn(n, carry):
        g, k = n // C, n % C
        if aligned:

            @pl.when(n < C)
            def _():
                for copy in load_kv(k):
                    copy.wait()

        unit(g, k)

        @pl.when(n == 0)
        def _():
            pl.semaphore_wait(barrier, 2 * C + H - 2)

        @pl.when(k < C - 1)
        def _():
            for copy in a_copies(g, k):
                copy.start()

        @pl.when(n == C)
        def _():
            load_w().wait()
            combine(0)
            outgoing(0)

        @pl.when(n > C)
        def _():
            pass_on(0, (k - 1) * C // (C - 1), k * C // (C - 1))

        return carry

    lax.fori_loop(0, 2 * C, turn, 0)
    combine(1)
    outgoing(1)
    pass_on(1, 0, C)

    for g in range(2):
        result = jnp.zeros((half, width), jnp.float32)
        for k in range(C):
            z_copy(g, k).wait()
            result = result + z_recv[g, k].astype(jnp.float32)
        out_ref[g * half : (g + 1) * half, :] = result.astype(out_ref.dtype)


def on_device(queries, keys, values, lengths, selected, out_weight):
    S, C, H = lax.axis_size("segment"), lax.axis_size("ctx"), lax.axis_size("head")
    rows, q_cols = queries.shape
    span, kv_cols = keys.shape
    kv_count = kv_cols // HEAD_DIM
    depth, d = out_weight.shape
    width = d // (C * H)
    half = rows // 2
    stat_rows = -(-2 * (depth // HEAD_DIM) // 8) * 8
    whole = pl.BlockSpec(memory_space=pl.ANY)
    scalars = pl.BlockSpec(memory_space=pltpu.SMEM)
    wire = jnp.bfloat16
    return pl.pallas_call(
        functools.partial(relay, (S, C, H)),
        out_shape=jax.ShapeDtypeStruct((rows, width), jnp.bfloat16),
        in_specs=[scalars, scalars, whole, whole, whole, whole],
        out_specs=pl.BlockSpec(memory_space=pltpu.VMEM),
        scratch_shapes=[
            pltpu.VMEM((rows, q_cols), queries.dtype),
            pltpu.VMEM((kv_count, span, HEAD_DIM), keys.dtype),
            pltpu.VMEM((kv_count, span, HEAD_DIM), values.dtype),
            pltpu.VMEM((depth, d), out_weight.dtype),
            pltpu.VMEM((8, span), jnp.float32),
            pltpu.VMEM((2, C, half, depth), wire),
            pltpu.VMEM((2, C - 1, half, depth), wire),
            pltpu.VMEM((2, C, stat_rows, HEAD_DIM), jnp.float32),
            pltpu.VMEM((2, C - 1, stat_rows, HEAD_DIM), jnp.float32),
            pltpu.VMEM((2, half, depth), wire),
            pltpu.VMEM((2, H - 1, C, half, width), wire),
            pltpu.VMEM((2, H - 1, C, half, width), wire),
            pltpu.VMEM((2, C, half, width), wire),
            pltpu.VMEM((2, C, half, width), wire),
            pltpu.SemaphoreType.DMA((2,)),
            pltpu.SemaphoreType.DMA((kv_count,)),
            pltpu.SemaphoreType.DMA((kv_count,)),
            pltpu.SemaphoreType.DMA((2, 2, C - 1)),
            pltpu.SemaphoreType.DMA((2, 2, C - 1)),
            pltpu.SemaphoreType.DMA((2, 2, H - 1, C)),
            pltpu.SemaphoreType.DMA((2, 2, C)),
        ],
        compiler_params=pltpu.CompilerParams(
            collective_id=0, has_side_effects=True, vmem_limit_bytes=58 * 2**20
        ),
        cost_estimate=pl.CostEstimate(
            flops=4 * rows * q_cols * span + 2 * rows * depth * d,
            bytes_accessed=2 * (rows * q_cols + 2 * span * kv_cols + depth * d),
            transcendentals=rows * q_cols // HEAD_DIM * span,
        ),
    )(lengths, selected, queries, keys, values, out_weight)


def solution(mesh):
    placed = (
        P("segment", "head"),
        P(("segment", "ctx"), "head"),
        P(("segment", "ctx"), "head"),
        P("segment"),
        P("segment", None),
        P(("head", "ctx"), None),
    )
    return jax.shard_map(
        on_device,
        mesh=mesh,
        in_specs=placed,
        out_specs=P("segment", ("head", "ctx")),
        check_vma=False,
    )
```

time: 91.8 us -> 68.2 us (0.74); the launches traced: 90.5 us -> 68 us
  Pallas kernels: 88.2 us -> 65.7 us
    pallas_call x1, Pallas kernels: 88.2 us -> 65.7 us  [on_device(): pl.pallas_call(functools.partial(relay, (S, C, H)), out_shape=jax.ShapeDt...]
where the time goes in v2:
time: 68.2 us; the launch traced here: 68 us
  Pallas kernels  65.7 us (96%)
  local copies, waits for them, and re-layouts  1.67 us (2%)
    pallas_call x1, Pallas kernels, on_device(): pl.pallas_call(functools.partial(relay, (S, C, H)), out_shape=jax.ShapeDt...  65.7 us
    unnamed x1, local copies, waits for them, and re-layouts  1.67 us

profile of v2, /device:TPU:1, one launch (start us, length us, event | category | flops | bytes accessed | tf_op | source)
XLA Modules:
  0.0 68.0 jit_solution(11860910139231538793)
XLA Ops:
  0.7 65.7 %shard_map.64 = bf16[128,1024]{1,0:T(8,128)(2,1)} custom-call(s32[1]{0:T(128)S(6)} %copy.8.length_ref, s32[1,3]{1,0:T(1,128)} %chosen_ref.1, bf16[128,4096]{1,0:T(8,128)(2,1)} %q_hbm.1, bf16[4096,512]{1,0:T(8,128)(2,1)} %k_hbm.1, bf16[4096,512]{1,0:T(8,128)(2,1)} %v_hbm.1, bf16[1024,8192]{1,0:T(8,128)(2,1)} %w_hbm.1), custom_call_target="tpu_custom_call" | custom-call | flops 10737418240 | bytes 26214400 | tf_op jit(solution)/shard_map/pallas_call | solution.py:297
  66.3 1.7 %copy.9 = bf16[128,1024]{1,0:T(8,128)(2,1)} copy(bf16[128,1024]{1,0:T(8,128)(2,1)} %shard_map.64) | data formatting | bytes 524288

commit v3 on v2

--- a/solution.py
+++ b/solution.py
@@ -127,9 +127,11 @@
         slot = k if aligned else (owner * per_ctx) // group
         own_rows = pl.ds(pl.multiple_of(g * half, half), half)
         tiles = per_ctx // together
-        scores = []
-        for t in range(tiles):
-            q = jnp.concatenate(
+        chunk = 2 * HEAD_DIM
+        pieces = [slice(first, first + chunk) for first in range(0, span, chunk)]
+
+        def rows_of(t):
+            return jnp.concatenate(
                 [
                     q_buf[
                         own_rows,
@@ -144,19 +146,37 @@
                 ],
                 axis=0,
             )
-            scores.append(
-                lax.dot_general(
-                    q, k_buf[slot], (((1,), (1,)), ((), ())), preferred_element_type=jnp.float32
-                )
-                + bias[0:1, :]
+
+        def score(q, high, piece):
+            block = bias[0:1, piece] + lax.dot_general(
+                q, k_buf[slot, piece, :], (((1,), (1,)), ((), ())),
+                preferred_element_type=jnp.float32,
             )
+            for first in range(0, chunk, HEAD_DIM):
+                high = jnp.maximum(high, block[:, first : first + HEAD_DIM])
+            return high, block
+
+        floor = jnp.full((together * half, HEAD_DIM), FLOOR, jnp.float32)
+        q, high, blocks = rows_of(0), floor, []
+        for piece in pieces:
+            high, block = score(q, high, piece)
+            blocks.append(block)
         stats = jnp.zeros((half, HEAD_DIM), jnp.float32)
         for t in range(tiles):
-            top = jnp.maximum(jnp.max(scores[t], axis=1, keepdims=True), FLOOR)
-            expo = jnp.exp2(scores[t] * UNITS - top * UNITS).astype(jnp.bfloat16)
+            top = jnp.max(high, axis=1, keepdims=True)
+            level = top * UNITS
+            later, expos = [], []
+            if t + 1 < tiles:
+                q, high = rows_of(t + 1), floor
+            for piece, block in zip(pieces, blocks):
+                if t + 1 < tiles:
+                    high, ahead = score(q, high, piece)
+                    later.append(ahead)
+                expos.append(jnp.exp2(block * UNITS - level).astype(jnp.bfloat16))
+            blocks = later
             ones = jnp.ones((span, HEAD_DIM), jnp.bfloat16)
             summed = jnp.dot(
-                expo,
+                jnp.concatenate(expos, axis=1),
                 jnp.concatenate([v_buf[slot], ones], axis=1),
                 preferred_element_type=jnp.float32,
             )

time: 68.2 us -> 68.7 us (level)
  no operation moved by 1% of the time
where the time goes in v3:
time: 68.7 us; the launch traced here: 68.5 us
  Pallas kernels  66.2 us (96%)
  local copies, waits for them, and re-layouts  1.67 us (2%)
    pallas_call x1, Pallas kernels, on_device(): pl.pallas_call(functools.partial(relay, (S, C, H)), out_shape=jax.ShapeDt...  66.2 us
    unnamed x1, local copies, waits for them, and re-layouts  1.67 us

profile of v3, /device:TPU:1, one launch (start us, length us, event | category | flops | bytes accessed | tf_op | source)
XLA Modules:
  0.0 68.5 jit_solution(3378014477721677948)
XLA Ops:
  0.7 66.2 %shard_map.64 = bf16[128,1024]{1,0:T(8,128)(2,1)} custom-call(s32[1]{0:T(128)S(6)} %copy.8.length_ref, s32[1,3]{1,0:T(1,128)} %chosen_ref.1, bf16[128,4096]{1,0:T(8,128)(2,1)} %q_hbm.1, bf16[4096,512]{1,0:T(8,128)(2,1)} %k_hbm.1, bf16[4096,512]{1,0:T(8,128)(2,1)} %v_hbm.1, bf16[1024,8192]{1,0:T(8,128)(2,1)} %w_hbm.1), custom_call_target="tpu_custom_call" | custom-call | flops 10737418240 | bytes 26214400 | tf_op jit(solution)/shard_map/pallas_call | solution.py:317
  66.8 1.7 %copy.9 = bf16[128,1024]{1,0:T(8,128)(2,1)} copy(bf16[128,1024]{1,0:T(8,128)(2,1)} %shard_map.64) | data formatting | bytes 524288

commit v4 on v2

--- a/solution.py
+++ b/solution.py
@@ -53,7 +53,7 @@
     kv_count, span, _ = k_buf.shape
     per_ctx = q_cols // (HEAD_DIM * C)
     group = q_cols // (HEAD_DIM * kv_count)
-    together = math.gcd(per_ctx, 4)
+    together = math.gcd(per_ctx, 8)
     half = rows // 2
     width = out_ref.shape[1]
     stat_rows = t_send.shape[2]

time: 68.2 us -> 80.6 us (1.18)
  Pallas kernels: 65.7 us -> 78.1 us
    pallas_call x1, Pallas kernels: 65.7 us -> 78.1 us  [on_device(): pl.pallas_call(functools.partial(relay, (S, C, H)), out_shape=jax.ShapeDt...]
where the time goes in v4:
time: 80.6 us; the launch traced here: 80.4 us
  Pallas kernels  78.1 us (97%)
  local copies, waits for them, and re-layouts  1.67 us (2%)
    pallas_call x1, Pallas kernels, on_device(): pl.pallas_call(functools.partial(relay, (S, C, H)), out_shape=jax.ShapeDt...  78.1 us
    unnamed x1, local copies, waits for them, and re-layouts  1.67 us

profile of v4, /device:TPU:1, one launch (start us, length us, event | category | flops | bytes accessed | tf_op | source)
XLA Modules:
  0.0 80.4 jit_solution(16735687551463741188)
XLA Ops:
  0.7 78.1 %shard_map.64 = bf16[128,1024]{1,0:T(8,128)(2,1)} custom-call(s32[1]{0:T(128)S(6)} %copy.8.length_ref, s32[1,3]{1,0:T(1,128)} %chosen_ref.1, bf16[128,4096]{1,0:T(8,128)(2,1)} %q_hbm.1, bf16[4096,512]{1,0:T(8,128)(2,1)} %k_hbm.1, bf16[4096,512]{1,0:T(8,128)(2,1)} %v_hbm.1, bf16[1024,8192]{1,0:T(8,128)(2,1)} %w_hbm.1), custom_call_target="tpu_custom_call" | custom-call | flops 10737418240 | bytes 26214400 | tf_op jit(solution)/shard_map/pallas_call | solution.py:297
  78.8 1.7 %copy.9 = bf16[128,1024]{1,0:T(8,128)(2,1)} copy(bf16[128,1024]{1,0:T(8,128)(2,1)} %shard_map.64) | data formatting | bytes 524288
